TPU v7x, 128 devices: a whole 4x4x4 slice. The times are simulated.
128 devices in a mesh: shot: 8 (over y, core), tile: 16 (over z, x).
Axes of the slice: x: 4, y: 4, z: 4, core: 2. Of those that a mesh axis runs over, the one named last changes fastest.
Arguments:
- coefs: float32 [3, 16, 2048, 128], P(None, 'shot', 'tile')
- fwd_state: float32 [8, 4, 16, 2048, 128], P('shot', None, None, 'tile'), may hold values from -3 to 3
- adj_state: float32 [8, 4, 16, 2048, 128], P('shot', None, None, 'tile'), may hold values from -3 to 3
- src_cell: int32 [8, 16], P('shot', 'tile'), may hold values from 0 to 262143
- src_wave: float32 [8, 6], P('shot'), may hold values from -8 to 8
- rec_cells: int32 [8, 2048], P('shot', 'tile'), may hold values from 0 to 262143
- observed: float32 [8, 6, 2048], P('shot', None, 'tile'), may hold values from -6 to 6
Outputs:
- gradient: float32 [3, 16, 2048, 128], P(None, 'shot', 'tile')
- fwd_final: float32 [8, 2, 16, 2048, 128], P('shot', None, None, 'tile')
- adj_final: float32 [8, 2, 16, 2048, 128], P('shot', None, None, 'tile')
Inputs may be any that keep to these rules, and one draw needn't show every extreme that they name: `src_cell`: local cell index depth * 128 * 128 + first * 128 + second inside the aperture tile. `rec_cells`: local cell index inside the tile of the receiver's block; cells may repeat.
All inputs are finite; a program needn't handle non-finite values.
Results may differ from a plain program's by a relative error of at most 0.0003.
Values sent between devices are 32-bit elements; how exact they have to be, the bound alone decides.
A program may use at most 192 MiB of HBM per device.

v0:
```python
import functools

import jax
import jax.numpy as jnp
from jax import lax
from jax.experimental import pallas as pl
from jax.experimental.pallas import tpu as pltpu
from jax.sharding import PartitionSpec as P

MESH = pl.DeviceIdType.MESH
F32 = jnp.float32
AZ, AX, AY, STEPS, NREC = 16, 128, 128, 6, 128
PAD = 8
GROUPS, DEEP = 4, 4


def kernel(
    n_shot,
    n_tile,
    coefs,
    fwd_state,
    adj_state,
    src_cell,
    src_wave,
    rec_cells,
    rec_row,
    observed_in,
    gradient,
    fwd_final,
    adj_final,
    cf,
    pp,
    qq,
    hs,
    zs,
    ll,
    mm,
    ff,
    oo,
    acc,
    rb,
    ry,
    hb,
    sb,
    picks,
    gath,
    spread,
    inj,
    observed,
    load_sem,
    out_sem,
    halo_send,
    halo_recv,
    whole_send,
    whole_recv,
    ag_send,
    ag_recv,
    rs_send,
    rs_recv,
):
    shot = lax.axis_index("shot")
    tile = lax.axis_index("tile")
    chip = shot // 2
    core = shot % 2
    sibling = chip * 2 + (1 - core)
    up = (shot + 2) % n_shot
    down = (shot + n_shot - 2) % n_shot
    left = (tile + n_tile - 1) % n_tile
    right = (tile + 1) % n_tile
    has_left = tile > 0
    has_right = tile < n_tile - 1
    mine = 2 * shot
    mine_sib = 2 * sibling
    above = (mine + 4) % AZ
    below = (mine + 12) % AZ
    far = (mine + 8) % AZ
    above_sib = (mine_sib + 4) % AZ
    below_sib = (mine_sib + 12) % AZ
    far_sib = (mine_sib + 8) % AZ

    own_load = pltpu.make_async_copy(coefs, cf.at[:, pl.ds(mine, 2)], load_sem.at[0])
    own_load.start()
    observed_load = pltpu.make_async_copy(observed_in, observed, load_sem.at[9])
    observed_load.start()
    body = pl.ds(PAD, AX)
    loads = []
    for i, (src, dst) in enumerate(
        (
            (fwd_state.at[0, 0], pp.at[0:AZ, body]),
            (fwd_state.at[0, 1], qq.at[2 : AZ + 2]),
            (fwd_state.at[0, 2], pp.at[AZ : 2 * AZ, body]),
            (fwd_state.at[0, 3], qq.at[AZ + 6 : 2 * AZ + 6]),
            (adj_state.at[0, 0], ll.at[0:AZ]),
            (adj_state.at[0, 1], mm.at[0:AZ]),
            (adj_state.at[0, 2], ll.at[AZ : 2 * AZ]),
            (adj_state.at[0, 3], mm.at[AZ : 2 * AZ]),
        )
    ):
        loads.append(pltpu.make_async_copy(src, dst, load_sem.at[1 + i]))

    def clear(i, carry):
        hb[pl.ds(i * 32, 32)] = jnp.zeros((32, AY), F32)
        return carry

    lax.fori_loop(0, 12, clear, 0)

    barrier = pltpu.get_barrier_semaphore()
    for other in (sibling, up, down):
        pl.semaphore_signal(barrier, inc=1, device_id=(other, tile), device_id_type=MESH)

    @pl.when(has_left)
    def _():
        pl.semaphore_signal(barrier, inc=1, device_id=(shot, left), device_id_type=MESH)

    @pl.when(has_right)
    def _():
        pl.semaphore_signal(barrier, inc=1, device_id=(shot, right), device_id_type=MESH)

    for copy in loads:
        copy.start()
    own_load.wait()
    cf[0, pl.ds(mine, 2)] = cf[0, pl.ds(mine, 2)] * F32(1.0 / 12.0)

    pl.semaphore_wait(barrier, 3 + jnp.minimum(tile, 1) + jnp.minimum(n_tile - 1 - tile, 1))

    def ag(index, layer, count, target):
        part = cf.at[:, pl.ds(layer, count)]
        return pltpu.make_async_remote_copy(
            src_ref=part,
            dst_ref=part,
            send_sem=ag_send.at[index],
            recv_sem=ag_recv.at[index],
            device_id=(target, tile),
            device_id_type=MESH,
        )

    send_up0 = ag(1, mine, 1, up)
    send_up1 = ag(2, mine + 1, 1, up)
    send_down0 = ag(3, mine + 1, 1, down)
    send_down1 = ag(4, mine, 1, down)
    send_sib = ag(0, mine, 2, sibling)
    for copy in (send_up0, send_down0, send_up1, send_down1, send_sib):
        copy.start()
    got_up0 = ag(1, below, 1, up)
    got_up1 = ag(2, below + 1, 1, up)
    got_down0 = ag(3, above + 1, 1, down)
    got_down1 = ag(4, above, 1, down)
    hop_up = ag(5, below, 1, up)
    hop_down = ag(6, above + 1, 1, down)
    got_hop_up = ag(5, far, 1, up)
    got_hop_down = ag(6, far + 1, 1, down)
    got_sib = ag(0, mine_sib, 2, sibling)
    pass_up0 = ag(7, below, 1, sibling)
    pass_down0 = ag(8, above + 1, 1, sibling)
    pass_up1 = ag(9, below + 1, 1, sibling)
    pass_down1 = ag(10, above, 1, sibling)
    pass_far0 = ag(11, far, 1, sibling)
    pass_far1 = ag(12, far + 1, 1, sibling)
    via_up0 = ag(7, below_sib, 1, sibling)
    via_down0 = ag(8, above_sib + 1, 1, sibling)
    via_up1 = ag(9, below_sib + 1, 1, sibling)
    via_down1 = ag(10, above_sib, 1, sibling)
    via_far0 = ag(11, far_sib, 1, sibling)
    via_far1 = ag(12, far_sib + 1, 1, sibling)

    none = jnp.zeros((AX, AY), F32)
    for base in (0, AZ + 4):
        for extra in (0, 1, AZ + 2, AZ + 3):
            qq[base + extra] = none
            oo[base + extra] = none

    marked = rec_row[...] >> 7
    gap = lax.broadcasted_iota(jnp.int32, (AY, AY), 0) - lax.broadcasted_iota(jnp.int32, (AY, AY), 1)
    gap = gap * gap
    taps = jnp.where(gap == 0, F32(-60), F32(0)) + jnp.where(gap == 1, F32(16), F32(0)) - jnp.where(gap == 4, F32(1), F32(0))
    taps = taps.astype(jnp.bfloat16)
    spread[2 * NREC : 3 * NREC] = taps
    spread[3 * NREC : 4 * NREC] = taps

    def mark(i, carry):
        rows = lax.broadcasted_iota(jnp.int32, (16, NREC), 0) + i * 16
        hit = jnp.where(rows == marked, F32(1.0), F32(0.0)).astype(jnp.bfloat16)
        at = pl.ds(pl.multiple_of(i * 16, 16), 16)
        picks[at, 0:NREC] = hit
        picks[at, NREC : 2 * NREC] = hit
        return carry

    lax.fori_loop(0, AZ * AX // 16, mark, 0)

    def halo(slot, group, to_right):
        src = sb.at[pl.ds((1 if to_right else 0) * 192 + slot * 32 + group * 8, 8)]
        dst = hb.at[pl.ds((0 if to_right else 1) * 192 + slot * 32 + group * 8, 8)]
        side = 0 if to_right else 1
        return pltpu.make_async_remote_copy(
            src_ref=src,
            dst_ref=dst,
            send_sem=halo_send.at[side, slot, group],
            recv_sem=halo_recv.at[side, slot, group],
            device_id=(shot, right if to_right else left),
            device_id_type=MESH,
        )

    def whole(slot, index, to_right):
        src = sb.at[pl.ds((1 if to_right else 0) * 192 + slot * 32, 32)]
        dst = hb.at[pl.ds((0 if to_right else 1) * 192 + slot * 32, 32)]
        side = 0 if to_right else 1
        return pltpu.make_async_remote_copy(
            src_ref=src,
            dst_ref=dst,
            send_sem=whole_send.at[side, index],
            recv_sem=whole_recv.at[side, index],
            device_id=(shot, right if to_right else left),
            device_id_type=MESH,
        )

    def both(build, act_left, act_right):
        @pl.when(has_left)
        def _():
            act_left(build)

        @pl.when(has_right)
        def _():
            act_right(build)

    def start(build):
        both(build, lambda b: b(False).start(), lambda b: b(True).start())

    def wait_send(build):
        both(build, lambda b: b(False).wait_send(), lambda b: b(True).wait_send())

    def wait_recv(build):
        both(build, lambda b: b(True).wait_recv(), lambda b: b(False).wait_recv())

    def stage_rows(field, at, slot, layer):
        sb[pl.ds(slot * 32 + layer * 2, 2)] = field[at, PAD : PAD + 2]
        sb[pl.ds(192 + slot * 32 + layer * 2, 2)] = field[at, PAD + AX - 2 : PAD + AX]

    def land_rows(field, at, slot, layer):
        field[at, PAD - 2 : PAD] = hb[pl.ds(slot * 32 + layer * 2, 2)]
        field[at, PAD + AX : PAD + AX + 2] = hb[pl.ds(192 + slot * 32 + layer * 2, 2)]

    loads[0].wait()

    def stage_first(d, carry):
        stage_rows(pp, d, 3, d)
        return carry

    lax.fori_loop(0, AZ, stage_first, 0)
    start(functools.partial(whole, 3, 0))

    lane = lax.broadcasted_iota(jnp.int32, (8, AY), 1)
    flat = lax.broadcasted_iota(jnp.int32, (8, AY), 0) * AY + lane

    def lap(field, at, r):
        def rows(k):
            return field[at, r + k : r + k + 8]

        one = rows(-1) + rows(1)
        two = rows(-2) + rows(2)
        return F32(16) * one - two

    def flat_terms(field, at, d):
        value = field[at, PAD : PAD + AX]
        high = value.astype(jnp.bfloat16)
        low = (value - high.astype(F32)).astype(jnp.bfloat16)
        if d is None:
            left_side = jnp.concatenate([high, low], axis=1)
            inj[...] = jnp.dot(left_side, spread[2 * NREC : 4 * NREC], preferred_element_type=F32)
        else:
            hits = picks[pl.ds(pl.multiple_of(d * AX, AX), AX)]
            left_side = jnp.concatenate([hits, high, low], axis=1)
            inj[...] = jnp.dot(left_side, spread[...], preferred_element_type=F32)

    def deep(field, at, r):
        def layer(k):
            return field[at + k, r : r + 8]

        return F32(16) * (layer(1) + layer(3)) - (layer(0) + layer(4)) - F32(30) * layer(2)

    def unrolled(fn):
        for t in range(AX // 8):
            fn(t)

    source = src_cell[0, 0]

    def gather_row(slot, parity, r, at_obs):
        cell = rec_cells[0, r]
        col = cell & (AY - 1)
        line = pp[parity * AZ + (cell >> 14), pl.ds(PAD + ((cell >> 7) & (AX - 1)), 1)]
        line = line - observed[0, at_obs, r]
        gath[slot, pl.ds(r, 1)] = jnp.where(lane[0:1] == col, line, F32(0))

    def forward_layer(n, cur, d, slot, order):
        nxt = 1 - cur
        here = cur * AZ + d
        there = nxt * AZ + d
        q_here = cur * (AZ + 4) + d
        q_there = nxt * (AZ + 4) + d + 2
        land_rows(pp, here, slot, d)
        wave = src_wave[0, n]
        start_cell = source - d * (AX * AY)
        obs_at = jnp.maximum(n - 1, 0)
        for j in range(8):
            gather_row(n, cur, order * 8 + j, obs_at)

        flat_terms(pp, here, None)

        def one(t):
            r = PAD + 8 * t
            c = cf[0, d, 8 * t : 8 * t + 8]
            a = cf[1, d, 8 * t : 8 * t + 8]
            b = cf[2, d, 8 * t : 8 * t + 8]
            h = lap(pp, here, r) + inj[8 * t : 8 * t + 8]
            z = deep(qq, q_here, 8 * t)
            hs[n * AZ + d, 8 * t : 8 * t + 8] = h
            zs[n * AZ + d, 8 * t : 8 * t + 8] = z
            pulse = jnp.where(flat == start_cell - 1024 * t, wave, F32(0))
            p = pp[here, r : r + 8]
            q = qq[q_here + 2, 8 * t : 8 * t + 8]
            p_new = (p + p) - pp[there, r : r + 8] + c * (a * h + b * z) + pulse
            q_new = (q + q) - qq[q_there, 8 * t : 8 * t + 8] + c * (b * h + z) + pulse
            pp[there, r : r + 8] = p_new
            qq[q_there, 8 * t : 8 * t + 8] = q_new

        unrolled(one)

    def scaled_layer(parity, d):
        def one(t):
            r = PAD + 8 * t
            at = pl.ds(8 * t, 8)
            c = cf[0, d, at]
            a = cf[1, d, at]
            b = cf[2, d, at]
            lam = ll[parity * AZ + d, at]
            mu = mm[parity * AZ + d, at]
            ff[parity * AZ + d, r : r + 8] = c * (a * lam + b * mu)
            oo[parity * (AZ + 4) + d + 2, at] = c * (b * lam + mu)

        unrolled(one)

    def ring_place(i):
        return (chip + i + i // 2 - 2 * (i // 3)) % GROUPS

    observed_load.wait()

    for i in range(1, 8):
        loads[i].wait()
    wait_recv(functools.partial(whole, 3, 0))
    got_sib.wait_recv()
    for i in range(GROUPS):
        if i == 1:
            got_up0.wait_recv()
            hop_up.start()
            pass_up0.start()
            got_down0.wait_recv()
            hop_down.start()
            pass_down0.start()
            got_up1.wait_recv()
            pass_up1.start()
            got_down1.wait_recv()
            pass_down1.start()
            via_down0.wait_recv()
            via_down1.wait_recv()
        if i == 2:
            via_up0.wait_recv()
            via_up1.wait_recv()
        if i == 3:
            got_hop_up.wait_recv()
            pass_far0.start()
            got_hop_down.wait_recv()
            pass_far1.start()
            via_far0.wait_recv()
            via_far1.wait_recv()
        group = ring_place(i)

        def layer0(j, carry, group=group, i=i):
            d = group * DEEP + j
            forward_layer(0, 0, d, 3, i * DEEP + j)
            stage_rows(pp, AZ + d, 1, d)
            scaled_layer(0, d)
            stage_rows(ff, d, 2, d)
            return carry

        lax.fori_loop(0, DEEP, layer0, 0)
        start(functools.partial(halo, 1, group))
    start(functools.partial(whole, 2, 1))

    def forward_step(n, carry):
        cur = n % 2

        def one_group(i, carry):
            group = ring_place(i)
            wait_recv(functools.partial(halo, cur, group))
            wait_send(functools.partial(halo, cur, group))

            def one_layer(j, carry):
                d = group * DEEP + j
                forward_layer(n, cur, d, cur, i * DEEP + j)
                stage_rows(pp, (1 - cur) * AZ + d, 1 - cur, d)
                return carry

            lax.fori_loop(0, DEEP, one_layer, 0)

            @pl.when(n < STEPS - 1)
            def _():
                start(functools.partial(halo, 1 - cur, group))

            return carry

        lax.fori_loop(0, GROUPS, one_group, 0)
        return carry

    lax.fori_loop(1, STEPS, forward_step, 0)

    out_p = pltpu.make_async_copy(pp.at[0:AZ, body], fwd_final.at[0, 0], out_sem.at[0])
    out_q = pltpu.make_async_copy(qq.at[2 : AZ + 2], fwd_final.at[0, 1], out_sem.at[1])
    out_p.start()
    out_q.start()

    def gather_last(i, carry):
        for j in range(8):
            gather_row(STEPS, 0, i * 8 + j, STEPS - 1)
        return carry

    lax.fori_loop(0, NREC // 8, gather_last, 0)

    def adj_layer(s, cur, d, slot, mode):
        nxt = 1 - cur
        here = cur * AZ + d
        there = nxt * AZ + d
        o_here = cur * (AZ + 4) + d
        o_there = nxt * (AZ + 4) + d + 2
        k = STEPS - s
        land_rows(ff, here, slot, d)
        flat_terms(ff, here, d)

        def one(t):
            r = PAD + 8 * t
            at = pl.ds(8 * t, 8)
            lam = ll[here, at]
            mu = mm[here, at]
            lam_old = ll[there, at]
            mu_old = mm[there, at]
            lam_new = inj[at] + (lam + lam) - lam_old + lap(ff, here, r)
            mu_new = (mu + mu) - mu_old + deep(oo, o_here, 8 * t)
            ll[there, at] = lam_new
            mm[there, at] = mu_new
            if mode != "last":
                c = cf[0, d, at]
                a = cf[1, d, at]
                b = cf[2, d, at]
                ff[there, r : r + 8] = c * (a * lam_new + b * mu_new)
                oo[o_there, at] = c * (b * lam_new + mu_new)
            if mode != "plain":
                h0 = hs[(k - 1) * AZ + d, at]
                z0 = zs[(k - 1) * AZ + d, at]
                h1 = hs[k * AZ + d, at]
                z1 = zs[k * AZ + d, at]
                h2 = hs[(k + 1) * AZ + d, at]
                z2 = zs[(k + 1) * AZ + d, at]
                q_h = lam_new * h0 + lam * h1 + lam_old * h2
                q_x = (lam_new * z0 + mu_new * h0) + (lam * z1 + mu * h1) + (lam_old * z2 + mu_old * h2)
                q_z = mu_new * z0 + mu * z1 + mu_old * z2
                if mode == "last":
                    q_h += acc[0, d, at]
                    q_x += acc[1, d, at]
                    q_z += acc[2, d, at]
                acc[0, d, at] = q_h
                acc[1, d, at] = q_x
                acc[2, d, at] = q_z

        unrolled(one)

    def set_spread(k):
        value = gath[k]
        high = value.astype(jnp.bfloat16)
        spread[0:NREC] = high
        spread[NREC : 2 * NREC] = (value - high.astype(F32)).astype(jnp.bfloat16)

    def adj_step(s, first, mode, carry):
        cur = s % 2
        slot = 2 if first else 4 + cur
        set_spread(STEPS - s)

        def one_group(i, carry):
            group = ring_place(i)
            if not first:
                wait_recv(functools.partial(halo, slot, group))
                wait_send(functools.partial(halo, slot, group))

            def one_layer(j, carry):
                d = group * DEEP + j
                adj_layer(s, cur, d, slot, mode)
                stage_rows(ff, (1 - cur) * AZ + d, 5 - cur, d)
                return carry

            lax.fori_loop(0, DEEP, one_layer, 0)
            start(functools.partial(halo, 5 - cur, group))
            return carry

        lax.fori_loop(0, GROUPS, one_group, 0)
        return carry

    wait_recv(functools.partial(whole, 2, 1))
    adj_step(0, True, "plain", 0)
    adj_step(1, False, "plain", 0)
    adj_step(2, False, "third", 0)
    lax.fori_loop(3, 5, lambda s, carry: adj_step(s, False, "plain", carry), 0)

    def exchange(i, group):
        layer = group * DEEP
        return pltpu.make_async_remote_copy(
            src_ref=acc.at[:, pl.ds(layer + 2 * (1 - core), 2)],
            dst_ref=rb.at[:, pl.ds(2 * i, 2)],
            send_sem=rs_send.at[i],
            recv_sem=rs_recv.at[i],
            device_id=(sibling, tile),
            device_id_type=MESH,
        )

    def ring(index, layer, target):
        return pltpu.make_async_remote_copy(
            src_ref=acc.at[:, pl.ds(layer, 1)],
            dst_ref=ry.at[:, pl.ds(index, 1)],
            send_sem=rs_send.at[4 + index],
            recv_sem=rs_recv.at[4 + index],
            device_id=(target, tile),
            device_id_type=MESH,
        )

    def add_pair(i, group):
        layer = group * DEEP + 2 * core

        def add(t, carry):
            at = pl.ds(pl.multiple_of(t * 16, 16), 16)
            for f in range(3):
                for e in range(2):
                    acc[f, layer + e, at] = acc[f, layer + e, at] + rb[f, 2 * i + e, at]
            return carry

        lax.fori_loop(0, AX // 16, add, 0)

    def add_hop(index, layer):
        def add(t, carry):
            at = pl.ds(pl.multiple_of(t * 16, 16), 16)
            for f in range(3):
                acc[f, layer, at] = acc[f, layer, at] + ry[f, index, at]
            return carry

        lax.fori_loop(0, AX // 16, add, 0)

    to_up0 = ring(0, far, up)
    to_down0 = ring(1, far + 1, down)
    to_up1 = ring(2, above + 1, up)
    to_down1 = ring(3, below, down)
    to_up2 = ring(4, above, up)
    to_down2 = ring(5, below + 1, down)

    set_spread(1)
    groups = [(chip + k) % GROUPS for k in (2, 3, 1, 0)]
    swaps = [exchange(i, groups[i]) for i in range(GROUPS)]

    def summed(i):
        swaps[i].wait_send()
        swaps[i].wait_recv()
        add_pair(i, groups[i])
        if i == 0:
            to_up0.start()
            to_down0.start()
        if i == 1:
            to_down1.start()
        if i == 2:
            to_up1.start()

    for i in range(GROUPS):
        group = groups[i]
        wait_recv(functools.partial(halo, 5, group))
        wait_send(functools.partial(halo, 5, group))

        def last_layer(j, carry, group=group):
            adj_layer(5, 1, group * DEEP + j, 5, "last")
            return carry

        lax.fori_loop(0, DEEP, last_layer, 0)
        swaps[i].start()
        if i > 0:
            summed(i - 1)
    out_l = pltpu.make_async_copy(ll.at[0:AZ], adj_final.at[0, 0], out_sem.at[2])
    out_m = pltpu.make_async_copy(mm.at[0:AZ], adj_final.at[0, 1], out_sem.at[3])
    out_l.start()
    out_m.start()
    summed(GROUPS - 1)
    to_up0.wait_recv()
    add_hop(0, above)
    to_up2.start()
    to_down0.wait_recv()
    add_hop(1, below + 1)
    to_down2.start()
    to_up1.wait_recv()
    to_down1.wait_recv()
    to_up2.wait_recv()
    to_down2.wait_recv()

    def finish(t, carry):
        at = pl.ds(pl.multiple_of(t * 16, 16), 16)
        for e, (direct, passed) in enumerate(((3, 4), (2, 5))):
            q_h, q_x, q_z = (
                acc[f, mine + e, at] + ry[f, direct, at] + ry[f, passed, at] for f in range(3)
            )
            c = cf[0, mine + e, at]
            a = cf[1, mine + e, at]
            b = cf[2, mine + e, at]
            gradient[0, e, at] = (a * q_h + b * q_x + q_z) * F32(1.0 / 12.0)
            gradient[1, e, at] = c * q_h
            gradient[2, e, at] = c * q_x
        return carry

    lax.fori_loop(0, AX // 16, finish, 0)

    for copy in (send_up0, send_down0, send_up1, send_down1, send_sib, hop_up, hop_down):
        copy.wait_send()
    for copy in (pass_up0, pass_down0, pass_up1, pass_down1, pass_far0, pass_far1):
        copy.wait_send()
    for copy in (to_up0, to_down0, to_up1, to_down1, to_up2, to_down2):
        copy.wait_send()
    wait_send(functools.partial(whole, 3, 0))
    wait_send(functools.partial(whole, 2, 1))
    out_p.wait()
    out_q.wait()
    out_l.wait()
    out_m.wait()


def solution(mesh):
    n_shot, n_tile = mesh.shape["shot"], mesh.shape["tile"]

    def per_device(coefs, fwd_state, adj_state, src_cell, src_wave, rec_cells, observed):
        hbm = pl.BlockSpec(memory_space=pl.ANY)
        smem = pl.BlockSpec(memory_space=pltpu.SMEM)
        vmem = pl.BlockSpec(memory_space=pltpu.VMEM)
        dma = pltpu.SemaphoreType.DMA
        return pl.pallas_call(
            functools.partial(kernel, n_shot, n_tile),
            out_shape=(
                jax.ShapeDtypeStruct((3, 2, AX, AY), F32),
                jax.ShapeDtypeStruct((1, 2, AZ, AX, AY), F32),
                jax.ShapeDtypeStruct((1, 2, AZ, AX, AY), F32),
            ),
            in_specs=[hbm, hbm, hbm, smem, smem, smem, vmem, hbm],
            out_specs=(vmem, hbm, hbm),
            scratch_shapes=[
                pltpu.VMEM((3, AZ, AX, AY), F32),
                pltpu.VMEM((2 * AZ, AX + 2 * PAD, AY), F32),
                pltpu.VMEM((2 * (AZ + 4), AX, AY), F32),
                pltpu.VMEM((STEPS * AZ, AX, AY), F32),
                pltpu.VMEM((STEPS * AZ, AX, AY), F32),
                pltpu.VMEM((2 * AZ, AX, AY), F32),
                pltpu.VMEM((2 * AZ, AX, AY), F32),
                pltpu.VMEM((2 * AZ, AX + 2 * PAD, AY), F32),
                pltpu.VMEM((2 * (AZ + 4), AX, AY), F32),
                pltpu.VMEM((3, AZ, AX, AY), F32),
                pltpu.VMEM((3, 8, AX, AY), F32),
                pltpu.VMEM((3, 6, AX, AY), F32),
                pltpu.VMEM((2 * 192, AY), F32),
                pltpu.VMEM((2 * 192, AY), F32),
                pltpu.VMEM((AZ * AX, 2 * NREC), jnp.bfloat16),
                pltpu.VMEM((STEPS + 1, NREC, AY), F32),
                pltpu.VMEM((4 * NREC, AY), jnp.bfloat16),
                pltpu.VMEM((AX, AY), F32),
                pltpu.SMEM((1, STEPS, NREC), F32),
                dma((10,)),
                dma((4,)),
                dma((2, 6, 4)),
                dma((2, 6, 4)),
                dma((2, 2)),
                dma((2, 2)),
                dma((13,)),
                dma((13,)),
                dma((10,)),
                dma((10,)),
            ],
            compiler_params=pltpu.CompilerParams(
                collective_id=0, has_side_effects=True, vmem_limit_bytes=56 * 1024 * 1024
            ),
        )(coefs, fwd_state, adj_state, src_cell, src_wave, rec_cells, rec_cells, observed)

    placed = (
        P(None, "shot", "tile", None),
        P("shot", None, None, "tile", None),
        P("shot", None, None, "tile", None),
        P("shot", "tile"),
        P("shot", None),
        P("shot", "tile"),
        P("shot", None, "tile"),
    )
    return jax.shard_map(
        per_device,
        mesh=mesh,
        in_specs=placed,
        out_specs=(
            P(None, "shot", "tile", None),
            P("shot", None, None, "tile", None),
            P("shot", None, None, "tile", None),
        ),
        check_vma=False,
    )
```

profile of v0, /device:TPU:96, one launch (start us, length us, event | category | flops | bytes accessed | tf_op | source)
XLA Modules:
  0.0 108.0 jit_solution(16660903228627320897)
XLA Ops:
  1.3 1.3 %copy.10.observed_in = f32[1,6,128]{2,1,0:T(8,128)} copy(f32[1,6,128]{2,0,1:T(1,128)} %param.13) | data formatting | bytes 6144 | tf_op args[6]
  2.6 99.0 %shard_map.94 = (f32[3,2,128,128]{3,2,1,0:T(8,128)}, f32[1,2,16,128,128]{4,3,2,1,0:T(8,128)}, f32[1,2,16,128,128]{4,3,2,1,0:T(8,128)}) custom-call(f32[3,2,128,128]{3,2,1,0:T(8,128)} %coefs.1, f32[1,4,16,128,128]{4,3,2,1,0:T(8,128)} %fwd_state.1, f32[1,4,16,128,128]{4,3,2,1,0:T(8,128)} %adj_state.1, s32[1,1]{1,0:T(1,128)S(6)} %copy.14.src_cell, ...), custom_call_target="tpu_custom_call" | custom-call | tf_op jit(solution)/shard_map/pallas_call | solution.py:642
  101.6 1.8 %copy.15 = f32[3,2,128,128]{3,2,1,0:T(8,128)} copy(f32[3,2,128,128]{3,2,1,0:T(8,128)} %get-tuple-element.6) | data formatting | bytes 786432
  103.4 0.0 copy-start
  103.4 3.3 %copy.16 = f32[1,2,16,128,128]{4,3,2,1,0:T(8,128)} copy(f32[1,2,16,128,128]{4,3,2,1,0:T(8,128)} %get-tuple-element.7) | data formatting | bytes 4194304
  106.6 0.0 copy-done
  106.6 1.3 %copy.17 = f32[1,2,16,128,128]{4,3,2,1,0:T(8,128)} copy(f32[1,2,16,128,128]{4,3,2,1,0:T(8,128)S(1)} %copy-done) | data formatting | bytes 4194304
Async XLA Ops:
  103.4 3.3 %copy-start = (f32[1,2,16,128,128]{4,3,2,1,0:T(8,128)S(1)}, f32[1,2,16,128,128]{4,3,2,1,0:T(8,128)}, u32[]{:S(2)}) copy-start(f32[1,2,16,128,128]{4,3,2,1,0:T(8,128)} %get-tuple-element.8) | copy-start | bytes 6291460
where the time goes:
time: 108 us
  Pallas kernels  99 us (92%)
  local copies, waits for them, and re-layouts  7.65 us (7%)
  between operations  1.29 us (1%)
    pallas_call x1, Pallas kernels, per_device(): pl.pallas_call(functools.partial(kernel, n_shot, n_tile), out_shape=(jax....  99 us
    unnamed x6, local copies, waits for them, and re-layouts  7.65 us

commit v1 on v0

--- a/solution.py
+++ b/solution.py
@@ -45,7 +45,8 @@
     picks,
     gath,
     spread,
-    inj,
+    terms_a,
+    terms_b,
     observed,
     load_sem,
     out_sem,
@@ -174,8 +175,8 @@
     gap = gap * gap
     taps = jnp.where(gap == 0, F32(-60), F32(0)) + jnp.where(gap == 1, F32(16), F32(0)) - jnp.where(gap == 4, F32(1), F32(0))
     taps = taps.astype(jnp.bfloat16)
-    spread[2 * NREC : 3 * NREC] = taps
-    spread[3 * NREC : 4 * NREC] = taps
+    for k in (2, 3, 6, 7):
+        spread[k * NREC : (k + 1) * NREC] = taps
 
     def mark(i, carry):
         rows = lax.broadcasted_iota(jnp.int32, (16, NREC), 0) + i * 16
@@ -248,107 +249,108 @@
     lax.fori_loop(0, AZ, stage_first, 0)
     start(functools.partial(whole, 3, 0))
 
-    lane = lax.broadcasted_iota(jnp.int32, (8, AY), 1)
-    flat = lax.broadcasted_iota(jnp.int32, (8, AY), 0) * AY + lane
+    lane = lax.broadcasted_iota(jnp.int32, (1, AY), 1)
+    flat = lax.broadcasted_iota(jnp.int32, (8, AY), 0) * AY + lax.broadcasted_iota(jnp.int32, (8, AY), 1)
+    source = src_cell[0, 0]
+
+    def ring_place(i):
+        return (chip + i + i // 2 - 2 * (i // 3)) % GROUPS
 
     def lap(field, at, r):
         def rows(k):
             return field[at, r + k : r + k + 8]
 
-        one = rows(-1) + rows(1)
-        two = rows(-2) + rows(2)
-        return F32(16) * one - two
-
-    def flat_terms(field, at, d):
-        value = field[at, PAD : PAD + AX]
+        return F32(16) * (rows(-1) + rows(1)) - (rows(-2) + rows(2))
+
+    def deep(layers):
+        return F32(16) * (layers[1] + layers[3]) - (layers[0] + layers[4]) - F32(30) * layers[2]
+
+    def flat_terms(field, parity, d, out, side):
+        value = field[pl.ds(parity * AZ + d, 2), PAD : PAD + AX].reshape(2 * AX, AY)
         high = value.astype(jnp.bfloat16)
         low = (value - high.astype(F32)).astype(jnp.bfloat16)
-        if d is None:
+        if side is None:
             left_side = jnp.concatenate([high, low], axis=1)
-            inj[...] = jnp.dot(left_side, spread[2 * NREC : 4 * NREC], preferred_element_type=F32)
+            out[...] = jnp.dot(left_side, spread[2 * NREC : 4 * NREC], preferred_element_type=F32)
         else:
-            hits = picks[pl.ds(pl.multiple_of(d * AX, AX), AX)]
+            hits = picks[pl.ds(pl.multiple_of(d * AX, AX), 2 * AX)]
             left_side = jnp.concatenate([hits, high, low], axis=1)
-            inj[...] = jnp.dot(left_side, spread[...], preferred_element_type=F32)
-
-    def deep(field, at, r):
-        def layer(k):
-            return field[at + k, r : r + 8]
-
-        return F32(16) * (layer(1) + layer(3)) - (layer(0) + layer(4)) - F32(30) * layer(2)
-
-    def unrolled(fn):
-        for t in range(AX // 8):
-            fn(t)
-
-    source = src_cell[0, 0]
+            right_side = spread[pl.ds(pl.multiple_of(side * 4 * NREC, 4 * NREC), 4 * NREC)]
+            out[...] = jnp.dot(left_side, right_side, preferred_element_type=F32)
 
     def gather_row(slot, parity, r, at_obs):
         cell = rec_cells[0, r]
         col = cell & (AY - 1)
         line = pp[parity * AZ + (cell >> 14), pl.ds(PAD + ((cell >> 7) & (AX - 1)), 1)]
-        line = line - observed[0, at_obs, r]
-        gath[slot, pl.ds(r, 1)] = jnp.where(lane[0:1] == col, line, F32(0))
-
-    def forward_layer(n, cur, d, slot, order):
+        line = line - observed[at_obs, 0, r]
+        gath[slot, pl.ds(r, 1)] = jnp.where(lane == col, line, F32(0))
+
+    def forward_pair(n, cur, d, terms):
         nxt = 1 - cur
         here = cur * AZ + d
         there = nxt * AZ + d
         q_here = cur * (AZ + 4) + d
         q_there = nxt * (AZ + 4) + d + 2
-        land_rows(pp, here, slot, d)
         wave = src_wave[0, n]
         start_cell = source - d * (AX * AY)
+        for t in range(AX // 8):
+            r = PAD + 8 * t
+            at = slice(8 * t, 8 * t + 8)
+            layers = [qq[q_here + k, at] for k in range(6)]
+            for e in range(2):
+                c = cf[0, d + e, at]
+                a = cf[1, d + e, at]
+                b = cf[2, d + e, at]
+                h = lap(pp, here + e, r) + terms[e * AX + 8 * t : e * AX + 8 * t + 8]
+                z = deep(layers[e : e + 5])
+                hs[n * AZ + d + e, at] = h
+                zs[n * AZ + d + e, at] = z
+                pulse = jnp.where(flat == start_cell - (AX * AY * e + 1024 * t), wave, F32(0))
+                p = pp[here + e, r : r + 8]
+                q = layers[e + 2]
+                pp[there + e, r : r + 8] = (p + p) - pp[there + e, r : r + 8] + c * (a * h + b * z) + pulse
+                qq[q_there + e, at] = (q + q) - qq[q_there + e, at] + c * (b * h + z) + pulse
+
+    def scaled_pair(d):
+        for t in range(AX // 8):
+            r = PAD + 8 * t
+            at = slice(8 * t, 8 * t + 8)
+            for e in range(2):
+                c = cf[0, d + e, at]
+                a = cf[1, d + e, at]
+                b = cf[2, d + e, at]
+                lam = ll[d + e, at]
+                mu = mm[d + e, at]
+                ff[d + e, r : r + 8] = c * (a * lam + b * mu)
+                oo[d + e + 2, at] = c * (b * lam + mu)
+
+    def forward_group(n, cur, i, group, slot):
+        d = group * DEEP
+        for e in range(DEEP):
+            land_rows(pp, cur * AZ + d + e, slot, d + e)
+        after = (cur + (i + 1) // GROUPS) % 2
         obs_at = jnp.maximum(n - 1, 0)
-        for j in range(8):
-            gather_row(n, cur, order * 8 + j, obs_at)
-
-        flat_terms(pp, here, None)
-
-        def one(t):
-            r = PAD + 8 * t
-            c = cf[0, d, 8 * t : 8 * t + 8]
-            a = cf[1, d, 8 * t : 8 * t + 8]
-            b = cf[2, d, 8 * t : 8 * t + 8]
-            h = lap(pp, here, r) + inj[8 * t : 8 * t + 8]
-            z = deep(qq, q_here, 8 * t)
-            hs[n * AZ + d, 8 * t : 8 * t + 8] = h
-            zs[n * AZ + d, 8 * t : 8 * t + 8] = z
-            pulse = jnp.where(flat == start_cell - 1024 * t, wave, F32(0))
-            p = pp[here, r : r + 8]
-            q = qq[q_here + 2, 8 * t : 8 * t + 8]
-            p_new = (p + p) - pp[there, r : r + 8] + c * (a * h + b * z) + pulse
-            q_new = (q + q) - qq[q_there, 8 * t : 8 * t + 8] + c * (b * h + z) + pulse
-            pp[there, r : r + 8] = p_new
-            qq[q_there, 8 * t : 8 * t + 8] = q_new
-
-        unrolled(one)
-
-    def scaled_layer(parity, d):
-        def one(t):
-            r = PAD + 8 * t
-            at = pl.ds(8 * t, 8)
-            c = cf[0, d, at]
-            a = cf[1, d, at]
-            b = cf[2, d, at]
-            lam = ll[parity * AZ + d, at]
-            mu = mm[parity * AZ + d, at]
-            ff[parity * AZ + d, r : r + 8] = c * (a * lam + b * mu)
-            oo[parity * (AZ + 4) + d + 2, at] = c * (b * lam + mu)
-
-        unrolled(one)
-
-    def ring_place(i):
-        return (chip + i + i // 2 - 2 * (i // 3)) % GROUPS
-
+        flat_terms(pp, cur, d + 2, terms_b, None)
+        for j in range(16):
+            gather_row(n, cur, i * 32 + j, obs_at)
+        forward_pair(n, cur, d, terms_a)
+        flat_terms(pp, after, ring_place((i + 1) % GROUPS) * DEEP, terms_a, None)
+        for j in range(16, 32):
+            gather_row(n, cur, i * 32 + j, obs_at)
+        forward_pair(n, cur, d + 2, terms_b)
+        for e in range(DEEP):
+            stage_rows(pp, (1 - cur) * AZ + d + e, 1 - cur, d + e)
+
+    flat_terms(pp, 0, ring_place(0) * DEEP, terms_a, None)
     observed_load.wait()
-
     for i in range(1, 8):
         loads[i].wait()
     wait_recv(functools.partial(whole, 3, 0))
     got_sib.wait_recv()
-    for i in range(GROUPS):
-        if i == 1:
+
+    def first_group(i, carry):
+        @pl.when(i == 1)
+        def _():
             got_up0.wait_recv()
             hop_up.start()
             pass_up0.start()
@@ -361,29 +363,33 @@
             pass_down1.start()
             via_down0.wait_recv()
             via_down1.wait_recv()
-        if i == 2:
+
+        @pl.when(i == 2)
+        def _():
             via_up0.wait_recv()
             via_up1.wait_recv()
-        if i == 3:
+
+        @pl.when(i == 3)
+        def _():
             got_hop_up.wait_recv()
             pass_far0.start()
             got_hop_down.wait_recv()
             pass_far1.start()
             via_far0.wait_recv()
             via_far1.wait_recv()
+
         group = ring_place(i)
-
-        def layer0(j, carry, group=group, i=i):
-            d = group * DEEP + j
-            forward_layer(0, 0, d, 3, i * DEEP + j)
-            stage_rows(pp, AZ + d, 1, d)
-            scaled_layer(0, d)
-            stage_rows(ff, d, 2, d)
-            return carry
-
-        lax.fori_loop(0, DEEP, layer0, 0)
+        d = group * DEEP
+        forward_group(0, 0, i, group, 3)
         start(functools.partial(halo, 1, group))
-    start(functools.partial(whole, 2, 1))
+        scaled_pair(d)
+        scaled_pair(d + 2)
+        for e in range(DEEP):
+            stage_rows(ff, d + e, 4, d + e)
+        start(functools.partial(halo, 4, group))
+        return carry
+
+    lax.fori_loop(0, GROUPS, first_group, 0)
 
     def forward_step(n, carry):
         cur = n % 2
@@ -392,14 +398,7 @@
             group = ring_place(i)
             wait_recv(functools.partial(halo, cur, group))
             wait_send(functools.partial(halo, cur, group))
-
-            def one_layer(j, carry):
-                d = group * DEEP + j
-                forward_layer(n, cur, d, cur, i * DEEP + j)
-                stage_rows(pp, (1 - cur) * AZ + d, 1 - cur, d)
-                return carry
-
-            lax.fori_loop(0, DEEP, one_layer, 0)
+            forward_group(n, cur, i, group, cur)
 
             @pl.when(n < STEPS - 1)
             def _():
@@ -418,94 +417,99 @@
     out_q.start()
 
     def gather_last(i, carry):
-        for j in range(8):
-            gather_row(STEPS, 0, i * 8 + j, STEPS - 1)
-        return carry
-
-    lax.fori_loop(0, NREC // 8, gather_last, 0)
-
-    def adj_layer(s, cur, d, slot, mode):
+        for j in range(16):
+            gather_row(STEPS, 0, i * 16 + j, STEPS - 1)
+        return carry
+
+    lax.fori_loop(0, NREC // 16, gather_last, 0)
+
+    def adj_pair(s, cur, d, terms, mode):
         nxt = 1 - cur
         here = cur * AZ + d
         there = nxt * AZ + d
         o_here = cur * (AZ + 4) + d
         o_there = nxt * (AZ + 4) + d + 2
         k = STEPS - s
-        land_rows(ff, here, slot, d)
-        flat_terms(ff, here, d)
-
-        def one(t):
+        for t in range(AX // 8):
             r = PAD + 8 * t
-            at = pl.ds(8 * t, 8)
-            lam = ll[here, at]
-            mu = mm[here, at]
-            lam_old = ll[there, at]
-            mu_old = mm[there, at]
-            lam_new = inj[at] + (lam + lam) - lam_old + lap(ff, here, r)
-            mu_new = (mu + mu) - mu_old + deep(oo, o_here, 8 * t)
-            ll[there, at] = lam_new
-            mm[there, at] = mu_new
-            if mode != "last":
-                c = cf[0, d, at]
-                a = cf[1, d, at]
-                b = cf[2, d, at]
-                ff[there, r : r + 8] = c * (a * lam_new + b * mu_new)
-                oo[o_there, at] = c * (b * lam_new + mu_new)
-            if mode != "plain":
-                h0 = hs[(k - 1) * AZ + d, at]
-                z0 = zs[(k - 1) * AZ + d, at]
-                h1 = hs[k * AZ + d, at]
-                z1 = zs[k * AZ + d, at]
-                h2 = hs[(k + 1) * AZ + d, at]
-                z2 = zs[(k + 1) * AZ + d, at]
-                q_h = lam_new * h0 + lam * h1 + lam_old * h2
-                q_x = (lam_new * z0 + mu_new * h0) + (lam * z1 + mu * h1) + (lam_old * z2 + mu_old * h2)
-                q_z = mu_new * z0 + mu * z1 + mu_old * z2
-                if mode == "last":
-                    q_h += acc[0, d, at]
-                    q_x += acc[1, d, at]
-                    q_z += acc[2, d, at]
-                acc[0, d, at] = q_h
-                acc[1, d, at] = q_x
-                acc[2, d, at] = q_z
-
-        unrolled(one)
-
-    def set_spread(k):
+            at = slice(8 * t, 8 * t + 8)
+            layers = [oo[o_here + n, at] for n in range(6)]
+            for e in range(2):
+                lam = ll[here + e, at]
+                mu = mm[here + e, at]
+                lam_old = ll[there + e, at]
+                mu_old = mm[there + e, at]
+                mix = terms[e * AX + 8 * t : e * AX + 8 * t + 8]
+                lam_new = (lam + lam) - lam_old + lap(ff, here + e, r) + mix
+                mu_new = (mu + mu) - mu_old + deep(layers[e : e + 5])
+                ll[there + e, at] = lam_new
+                mm[there + e, at] = mu_new
+                if mode != "last":
+                    c = cf[0, d + e, at]
+                    a = cf[1, d + e, at]
+                    b = cf[2, d + e, at]
+                    ff[there + e, r : r + 8] = c * (a * lam_new + b * mu_new)
+                    oo[o_there + e, at] = c * (b * lam_new + mu_new)
+                if mode != "plain":
+                    h0 = hs[(k - 1) * AZ + d + e, at]
+                    z0 = zs[(k - 1) * AZ + d + e, at]
+                    h1 = hs[k * AZ + d + e, at]
+                    z1 = zs[k * AZ + d + e, at]
+                    h2 = hs[(k + 1) * AZ + d + e, at]
+                    z2 = zs[(k + 1) * AZ + d + e, at]
+                    q_h = lam_new * h0 + lam * h1 + lam_old * h2
+                    q_x = (lam_new * z0 + mu_new * h0) + (lam * z1 + mu * h1) + (lam_old * z2 + mu_old * h2)
+                    q_z = mu_new * z0 + mu * z1 + mu_old * z2
+                    if mode == "last":
+                        q_h += acc[0, d + e, at]
+                        q_x += acc[1, d + e, at]
+                        q_z += acc[2, d + e, at]
+                    acc[0, d + e, at] = q_h
+                    acc[1, d + e, at] = q_x
+                    acc[2, d + e, at] = q_z
+
+    def set_spread(k, side):
         value = gath[k]
         high = value.astype(jnp.bfloat16)
-        spread[0:NREC] = high
-        spread[NREC : 2 * NREC] = (value - high.astype(F32)).astype(jnp.bfloat16)
-
-    def adj_step(s, first, mode, carry):
+        low = (value - high.astype(F32)).astype(jnp.bfloat16)
+        base = pl.multiple_of(side * 4 * NREC, 4 * NREC)
+        spread[pl.ds(base, 2 * NREC)] = jnp.concatenate([high, low], axis=0)
+
+    def last_place(i):
+        return (chip + 2 + i - 3 * (i // 2) - 2 * (i // 3)) % GROUPS
+
+    def adj_group(s, cur, i, mode, place):
+        group = place(i)
+        d = group * DEEP
+        slot = 4 + cur
+        wait_recv(functools.partial(halo, slot, group))
+        wait_send(functools.partial(halo, slot, group))
+        for e in range(DEEP):
+            land_rows(ff, cur * AZ + d + e, slot, d + e)
+        flat_terms(ff, cur, d + 2, terms_b, cur)
+        adj_pair(s, cur, d, terms_a, mode)
+        flat_terms(ff, cur, place((i + 1) % GROUPS) * DEEP, terms_a, cur)
+        adj_pair(s, cur, d + 2, terms_b, mode)
+        if mode != "last":
+            for e in range(DEEP):
+                stage_rows(ff, (1 - cur) * AZ + d + e, 5 - cur, d + e)
+            start(functools.partial(halo, 5 - cur, group))
+
+    def adj_step(s, mode, carry):
         cur = s % 2
-        slot = 2 if first else 4 + cur
-        set_spread(STEPS - s)
+        set_spread(STEPS - s, cur)
+        flat_terms(ff, cur, ring_place(0) * DEEP, terms_a, cur)
 
         def one_group(i, carry):
-            group = ring_place(i)
-            if not first:
-                wait_recv(functools.partial(halo, slot, group))
-                wait_send(functools.partial(halo, slot, group))
-
-            def one_layer(j, carry):
-                d = group * DEEP + j
-                adj_layer(s, cur, d, slot, mode)
-                stage_rows(ff, (1 - cur) * AZ + d, 5 - cur, d)
-                return carry
-
-            lax.fori_loop(0, DEEP, one_layer, 0)
-            start(functools.partial(halo, 5 - cur, group))
+            adj_group(s, cur, i, mode, ring_place)
             return carry
 
         lax.fori_loop(0, GROUPS, one_group, 0)
         return carry
 
-    wait_recv(functools.partial(whole, 2, 1))
-    adj_step(0, True, "plain", 0)
-    adj_step(1, False, "plain", 0)
-    adj_step(2, False, "third", 0)
-    lax.fori_loop(3, 5, lambda s, carry: adj_step(s, False, "plain", carry), 0)
+    lax.fori_loop(0, 2, lambda s, carry: adj_step(s, "plain", carry), 0)
+    adj_step(2, "third", 0)
+    lax.fori_loop(3, 5, lambda s, carry: adj_step(s, "plain", carry), 0)
 
     def exchange(i, group):
         layer = group * DEEP
@@ -556,35 +560,41 @@
     to_up2 = ring(4, above, up)
     to_down2 = ring(5, below + 1, down)
 
-    set_spread(1)
-    groups = [(chip + k) % GROUPS for k in (2, 3, 1, 0)]
-    swaps = [exchange(i, groups[i]) for i in range(GROUPS)]
+    set_spread(1, 1)
+    flat_terms(ff, 1, last_place(0) * DEEP, terms_a, 1)
+
+    def swap(i):
+        return exchange(i, last_place(i))
 
     def summed(i):
-        swaps[i].wait_send()
-        swaps[i].wait_recv()
-        add_pair(i, groups[i])
-        if i == 0:
+        swap(i).wait_send()
+        swap(i).wait_recv()
+        add_pair(i, last_place(i))
+
+    def last_group(i, carry):
+        adj_group(5, 1, i, "last", last_place)
+        swap(i).start()
+
+        @pl.when(i > 0)
+        def _():
+            summed(i - 1)
+
+        @pl.when(i == 1)
+        def _():
             to_up0.start()
             to_down0.start()
-        if i == 1:
+
+        @pl.when(i == 2)
+        def _():
             to_down1.start()
-        if i == 2:
+
+        @pl.when(i == 3)
+        def _():
             to_up1.start()
 
-    for i in range(GROUPS):
-        group = groups[i]
-        wait_recv(functools.partial(halo, 5, group))
-        wait_send(functools.partial(halo, 5, group))
-
-        def last_layer(j, carry, group=group):
-            adj_layer(5, 1, group * DEEP + j, 5, "last")
-            return carry
-
-        lax.fori_loop(0, DEEP, last_layer, 0)
-        swaps[i].start()
-        if i > 0:
-            summed(i - 1)
+        return carry
+
+    lax.fori_loop(0, GROUPS, last_group, 0)
     out_l = pltpu.make_async_copy(ll.at[0:AZ], adj_final.at[0, 0], out_sem.at[2])
     out_m = pltpu.make_async_copy(mm.at[0:AZ], adj_final.at[0, 1], out_sem.at[3])
     out_l.start()
@@ -624,7 +634,6 @@
     for copy in (to_up0, to_down0, to_up1, to_down1, to_up2, to_down2):
         copy.wait_send()
     wait_send(functools.partial(whole, 3, 0))
-    wait_send(functools.partial(whole, 2, 1))
     out_p.wait()
     out_q.wait()
     out_l.wait()
@@ -635,19 +644,19 @@
     n_shot, n_tile = mesh.shape["shot"], mesh.shape["tile"]
 
     def per_device(coefs, fwd_state, adj_state, src_cell, src_wave, rec_cells, observed):
-        hbm = pl.BlockSpec(memory_space=pl.ANY)
+        hbm = pl.BlockSpec(memory_space=pltpu.HBM)
         smem = pl.BlockSpec(memory_space=pltpu.SMEM)
         vmem = pl.BlockSpec(memory_space=pltpu.VMEM)
         dma = pltpu.SemaphoreType.DMA
         return pl.pallas_call(
             functools.partial(kernel, n_shot, n_tile),
             out_shape=(
-                jax.ShapeDtypeStruct((3, 2, AX, AY), F32),
-                jax.ShapeDtypeStruct((1, 2, AZ, AX, AY), F32),
-                jax.ShapeDtypeStruct((1, 2, AZ, AX, AY), F32),
+                pltpu.VMEM((3, 2, AX, AY), F32),
+                pltpu.VMEM((1, 2, AZ, AX, AY), F32),
+                pltpu.VMEM((1, 2, AZ, AX, AY), F32),
             ),
             in_specs=[hbm, hbm, hbm, smem, smem, smem, vmem, hbm],
-            out_specs=(vmem, hbm, hbm),
+            out_specs=(vmem, vmem, vmem),
             scratch_shapes=[
                 pltpu.VMEM((3, AZ, AX, AY), F32),
                 pltpu.VMEM((2 * AZ, AX + 2 * PAD, AY), F32),
@@ -665,15 +674,16 @@
                 pltpu.VMEM((2 * 192, AY), F32),
                 pltpu.VMEM((AZ * AX, 2 * NREC), jnp.bfloat16),
                 pltpu.VMEM((STEPS + 1, NREC, AY), F32),
-                pltpu.VMEM((4 * NREC, AY), jnp.bfloat16),
-                pltpu.VMEM((AX, AY), F32),
-                pltpu.SMEM((1, STEPS, NREC), F32),
+                pltpu.VMEM((8 * NREC, AY), jnp.bfloat16),
+                pltpu.VMEM((2 * AX, AY), F32),
+                pltpu.VMEM((2 * AX, AY), F32),
+                pltpu.SMEM((STEPS, 1, NREC), F32),
                 dma((10,)),
                 dma((4,)),
                 dma((2, 6, 4)),
                 dma((2, 6, 4)),
-                dma((2, 2)),
-                dma((2, 2)),
+                dma((2, 1)),
+                dma((2, 1)),
                 dma((13,)),
                 dma((13,)),
                 dma((10,)),
@@ -682,7 +692,7 @@
             compiler_params=pltpu.CompilerParams(
                 collective_id=0, has_side_effects=True, vmem_limit_bytes=56 * 1024 * 1024
             ),
-        )(coefs, fwd_state, adj_state, src_cell, src_wave, rec_cells, rec_cells, observed)
+        )(coefs, fwd_state, adj_state, src_cell, src_wave, rec_cells, rec_cells, observed.transpose(1, 0, 2))
 
     placed = (
         P(None, "shot", "tile", None),

time: 108 us -> 93.3 us (0.86)
  Pallas kernels: 99 us -> 88.5 us
  local copies, waits for them, and re-layouts: 7.65 us -> 3.39 us
    pallas_call x1, Pallas kernels: 99 us -> 88.5 us  [per_device(): pl.pallas_call(functools.partial(kernel, n_shot, n_tile), out_shape=(pltp...]
    unnamed x6 -> x3, local copies, waits for them, and re-layouts: 7.65 us -> 3.39 us
where the time goes in v1:
time: 93.3 us; the launch traced here: 93.2 us
  Pallas kernels  88.5 us (95%)
  local copies, waits for them, and re-layouts  3.39 us (4%)
  between operations  1.29 us (1%)
    pallas_call x1, Pallas kernels, per_device(): pl.pallas_call(functools.partial(kernel, n_shot, n_tile), out_shape=(pltp...  88.5 us
    unnamed x3, local copies, waits for them, and re-layouts  3.39 us

profile of v1, /device:TPU:96, one launch (start us, length us, event | category | flops | bytes accessed | tf_op | source)
XLA Modules:
  0.0 93.2 jit_solution(16224184796251562386)
XLA Ops:
  1.3 88.5 %shard_map.94 = (f32[3,2,128,128]{3,2,1,0:T(8,128)S(1)}, f32[1,2,16,128,128]{4,3,2,1,0:T(8,128)S(1)}, f32[1,2,16,128,128]{4,3,2,1,0:T(8,128)S(1)}) custom-call(f32[3,2,128,128]{3,2,1,0:T(8,128)} %coefs.1, f32[1,4,16,128,128]{4,3,2,1,0:T(8,128)} %fwd_state.1, f32[1,4,16,128,128]{4,3,2,1,0:T(8,128)} %adj_state.1, s32[1,1]{1,0:T(1,128)S(6)} %copy.16.src_cell, ...), custom_call_target="tpu_custom_call" | custom-call | tf_op jit(solution)/shard_map/pallas_call | solution.py:651
  89.8 0.7 copy.13
  90.6 1.3 %copy.14 = f32[1,2,16,128,128]{4,3,2,1,0:T(8,128)} copy(f32[1,2,16,128,128]{4,3,2,1,0:T(8,128)S(1)} %get-tuple-element.4) | data formatting | bytes 4194304
  91.9 1.3 %copy.15 = f32[1,2,16,128,128]{4,3,2,1,0:T(8,128)} copy(f32[1,2,16,128,128]{4,3,2,1,0:T(8,128)S(1)} %get-tuple-element.5) | data formatting | bytes 4194304

commit v2 on v1

--- a/solution.py
+++ b/solution.py
@@ -11,7 +11,9 @@
 F32 = jnp.float32
 AZ, AX, AY, STEPS, NREC = 16, 128, 128, 6, 128
 PAD = 8
-GROUPS, DEEP = 4, 4
+GROUPS, DEEP, BATCH, SENDS = 4, 4, 4, 4
+PER = GROUPS // SENDS
+SPAN = 8 * PER
 
 
 def kernel(
@@ -189,14 +191,26 @@
     lax.fori_loop(0, AZ * AX // 16, mark, 0)
 
     def halo(slot, group, to_right):
-        src = sb.at[pl.ds((1 if to_right else 0) * 192 + slot * 32 + group * 8, 8)]
-        dst = hb.at[pl.ds((0 if to_right else 1) * 192 + slot * 32 + group * 8, 8)]
+        src = sb.at[pl.ds((1 if to_right else 0) * 192 + slot * 32 + group * SPAN, SPAN)]
+        dst = hb.at[pl.ds((0 if to_right else 1) * 192 + slot * 32 + group * SPAN, SPAN)]
         side = 0 if to_right else 1
         return pltpu.make_async_remote_copy(
             src_ref=src,
             dst_ref=dst,
-            send_sem=halo_send.at[side, slot, group],
+            send_sem=halo_send.at[side, slot],
             recv_sem=halo_recv.at[side, slot, group],
+            device_id=(shot, right if to_right else left),
+            device_id_type=MESH,
+        )
+
+    def sent(slot, to_right):
+        rows = pl.ds((1 if to_right else 0) * 192 + slot * 32, 32)
+        side = 0 if to_right else 1
+        return pltpu.make_async_remote_copy(
+            src_ref=sb.at[rows],
+            dst_ref=hb.at[rows],
+            send_sem=halo_send.at[side, slot],
+            recv_sem=halo_recv.at[side, slot, 0],
             device_id=(shot, right if to_right else left),
             device_id_type=MESH,
         )
@@ -232,6 +246,16 @@
     def wait_recv(build):
         both(build, lambda b: b(True).wait_recv(), lambda b: b(False).wait_recv())
 
+    def ready(slot, i):
+        @pl.when(i % PER == PER - 1)
+        def _():
+            start(functools.partial(halo, slot, i // PER))
+
+    def arrived(slot, i):
+        @pl.when(i % PER == 0)
+        def _():
+            wait_recv(functools.partial(halo, slot, i // PER))
+
     def stage_rows(field, at, slot, layer):
         sb[pl.ds(slot * 32 + layer * 2, 2)] = field[at, PAD : PAD + 2]
         sb[pl.ds(192 + slot * 32 + layer * 2, 2)] = field[at, PAD + AX - 2 : PAD + AX]
@@ -242,8 +266,11 @@
 
     loads[0].wait()
 
-    def stage_first(d, carry):
-        stage_rows(pp, d, 3, d)
+    def ring_place(i):
+        return (chip + i + i // 2 - 2 * (i // 3)) % GROUPS
+
+    def stage_first(i, carry):
+        stage_rows(pp, ring_place(i // DEEP) * DEEP + i % DEEP, 3, i)
         return carry
 
     lax.fori_loop(0, AZ, stage_first, 0)
@@ -252,9 +279,6 @@
     lane = lax.broadcasted_iota(jnp.int32, (1, AY), 1)
     flat = lax.broadcasted_iota(jnp.int32, (8, AY), 0) * AY + lax.broadcasted_iota(jnp.int32, (8, AY), 1)
     source = src_cell[0, 0]
-
-    def ring_place(i):
-        return (chip + i + i // 2 - 2 * (i // 3)) % GROUPS
 
     def lap(field, at, r):
         def rows(k):
@@ -285,6 +309,12 @@
         line = line - observed[at_obs, 0, r]
         gath[slot, pl.ds(r, 1)] = jnp.where(lane == col, line, F32(0))
 
+    def flush(done, t):
+        if t % BATCH == BATCH - 1:
+            for field, layer, at, value in done:
+                field[layer, at] = value
+            done.clear()
+
     def forward_pair(n, cur, d, terms):
         nxt = 1 - cur
         here = cur * AZ + d
@@ -293,6 +323,7 @@
         q_there = nxt * (AZ + 4) + d + 2
         wave = src_wave[0, n]
         start_cell = source - d * (AX * AY)
+        done = []
         for t in range(AX // 8):
             r = PAD + 8 * t
             at = slice(8 * t, 8 * t + 8)
@@ -303,13 +334,16 @@
                 b = cf[2, d + e, at]
                 h = lap(pp, here + e, r) + terms[e * AX + 8 * t : e * AX + 8 * t + 8]
                 z = deep(layers[e : e + 5])
-                hs[n * AZ + d + e, at] = h
-                zs[n * AZ + d + e, at] = z
+                done.append((hs, n * AZ + d + e, at, h))
+                done.append((zs, n * AZ + d + e, at, z))
                 pulse = jnp.where(flat == start_cell - (AX * AY * e + 1024 * t), wave, F32(0))
                 p = pp[here + e, r : r + 8]
                 q = layers[e + 2]
-                pp[there + e, r : r + 8] = (p + p) - pp[there + e, r : r + 8] + c * (a * h + b * z) + pulse
-                qq[q_there + e, at] = (q + q) - qq[q_there + e, at] + c * (b * h + z) + pulse
+                p_new = (p + p) - pp[there + e, r : r + 8] + c * (a * h + b * z) + pulse
+                q_new = (q + q) - qq[q_there + e, at] + c * (b * h + z) + pulse
+                done.append((pp, there + e, slice(r, r + 8), p_new))
+                done.append((qq, q_there + e, at, q_new))
+            flush(done, t)
 
     def scaled_pair(d):
         for t in range(AX // 8):
@@ -327,7 +361,7 @@
     def forward_group(n, cur, i, group, slot):
         d = group * DEEP
         for e in range(DEEP):
-            land_rows(pp, cur * AZ + d + e, slot, d + e)
+            land_rows(pp, cur * AZ + d + e, slot, i * DEEP + e)
         after = (cur + (i + 1) // GROUPS) % 2
         obs_at = jnp.maximum(n - 1, 0)
         flat_terms(pp, cur, d + 2, terms_b, None)
@@ -339,7 +373,7 @@
             gather_row(n, cur, i * 32 + j, obs_at)
         forward_pair(n, cur, d + 2, terms_b)
         for e in range(DEEP):
-            stage_rows(pp, (1 - cur) * AZ + d + e, 1 - cur, d + e)
+            stage_rows(pp, (1 - cur) * AZ + d + e, 1 - cur, i * DEEP + e)
 
     flat_terms(pp, 0, ring_place(0) * DEEP, terms_a, None)
     observed_load.wait()
@@ -381,12 +415,12 @@
         group = ring_place(i)
         d = group * DEEP
         forward_group(0, 0, i, group, 3)
-        start(functools.partial(halo, 1, group))
+        ready(1, i)
         scaled_pair(d)
         scaled_pair(d + 2)
         for e in range(DEEP):
-            stage_rows(ff, d + e, 4, d + e)
-        start(functools.partial(halo, 4, group))
+            stage_rows(ff, d + e, 4, i * DEEP + e)
+        ready(4, i)
         return carry
 
     lax.fori_loop(0, GROUPS, first_group, 0)
@@ -396,17 +430,17 @@
 
         def one_group(i, carry):
             group = ring_place(i)
-            wait_recv(functools.partial(halo, cur, group))
-            wait_send(functools.partial(halo, cur, group))
+            arrived(cur, i)
             forward_group(n, cur, i, group, cur)
 
             @pl.when(n < STEPS - 1)
             def _():
-                start(functools.partial(halo, 1 - cur, group))
+                ready(1 - cur, i)
 
             return carry
 
         lax.fori_loop(0, GROUPS, one_group, 0)
+        wait_send(functools.partial(sent, cur))
         return carry
 
     lax.fori_loop(1, STEPS, forward_step, 0)
@@ -430,6 +464,7 @@
         o_here = cur * (AZ + 4) + d
         o_there = nxt * (AZ + 4) + d + 2
         k = STEPS - s
+        done = []
         for t in range(AX // 8):
             r = PAD + 8 * t
             at = slice(8 * t, 8 * t + 8)
@@ -442,14 +477,14 @@
                 mix = terms[e * AX + 8 * t : e * AX + 8 * t + 8]
                 lam_new = (lam + lam) - lam_old + lap(ff, here + e, r) + mix
                 mu_new = (mu + mu) - mu_old + deep(layers[e : e + 5])
-                ll[there + e, at] = lam_new
-                mm[there + e, at] = mu_new
+                done.append((ll, there + e, at, lam_new))
+                done.append((mm, there + e, at, mu_new))
                 if mode != "last":
                     c = cf[0, d + e, at]
                     a = cf[1, d + e, at]
                     b = cf[2, d + e, at]
-                    ff[there + e, r : r + 8] = c * (a * lam_new + b * mu_new)
-                    oo[o_there + e, at] = c * (b * lam_new + mu_new)
+                    done.append((ff, there + e, slice(r, r + 8), c * (a * lam_new + b * mu_new)))
+                    done.append((oo, o_there + e, at, c * (b * lam_new + mu_new)))
                 if mode != "plain":
                     h0 = hs[(k - 1) * AZ + d + e, at]
                     z0 = zs[(k - 1) * AZ + d + e, at]
@@ -464,9 +499,10 @@
                         q_h += acc[0, d + e, at]
                         q_x += acc[1, d + e, at]
                         q_z += acc[2, d + e, at]
-                    acc[0, d + e, at] = q_h
-                    acc[1, d + e, at] = q_x
-                    acc[2, d + e, at] = q_z
+                    done.append((acc.at[0], d + e, at, q_h))
+                    done.append((acc.at[1], d + e, at, q_x))
+                    done.append((acc.at[2], d + e, at, q_z))
+            flush(done, t)
 
     def set_spread(k, side):
         value = gath[k]
@@ -482,18 +518,22 @@
         group = place(i)
         d = group * DEEP
         slot = 4 + cur
-        wait_recv(functools.partial(halo, slot, group))
-        wait_send(functools.partial(halo, slot, group))
+        order = i if place is ring_place else GROUPS - 1 - i
+
+        @pl.when(i % PER == 0)
+        def _():
+            wait_recv(functools.partial(halo, slot, order // PER))
+
         for e in range(DEEP):
-            land_rows(ff, cur * AZ + d + e, slot, d + e)
+            land_rows(ff, cur * AZ + d + e, slot, order * DEEP + e)
         flat_terms(ff, cur, d + 2, terms_b, cur)
         adj_pair(s, cur, d, terms_a, mode)
         flat_terms(ff, cur, place((i + 1) % GROUPS) * DEEP, terms_a, cur)
         adj_pair(s, cur, d + 2, terms_b, mode)
         if mode != "last":
             for e in range(DEEP):
-                stage_rows(ff, (1 - cur) * AZ + d + e, 5 - cur, d + e)
-            start(functools.partial(halo, 5 - cur, group))
+                stage_rows(ff, (1 - cur) * AZ + d + e, 5 - cur, i * DEEP + e)
+            ready(5 - cur, i)
 
     def adj_step(s, mode, carry):
         cur = s % 2
@@ -505,6 +545,7 @@
             return carry
 
         lax.fori_loop(0, GROUPS, one_group, 0)
+        wait_send(functools.partial(sent, 4 + cur))
         return carry
 
     lax.fori_loop(0, 2, lambda s, carry: adj_step(s, "plain", carry), 0)
@@ -634,6 +675,7 @@
     for copy in (to_up0, to_down0, to_up1, to_down1, to_up2, to_down2):
         copy.wait_send()
     wait_send(functools.partial(whole, 3, 0))
+    wait_send(functools.partial(sent, 5))
     out_p.wait()
     out_q.wait()
     out_l.wait()
@@ -680,7 +722,7 @@
                 pltpu.SMEM((STEPS, 1, NREC), F32),
                 dma((10,)),
                 dma((4,)),
-                dma((2, 6, 4)),
+                dma((2, 6)),
                 dma((2, 6, 4)),
                 dma((2, 1)),
                 dma((2, 1)),

time: 93.3 us -> 87.2 us (0.935)
  Pallas kernels: 88.5 us -> 82.4 us
    pallas_call x1, Pallas kernels: 88.5 us -> 82.4 us  [per_device(): pl.pallas_call(functools.partial(kernel, n_shot, n_tile), out_shape=(pltp...]
where the time goes in v2:
time: 87.2 us; the launch traced here: 87 us
  Pallas kernels  82.4 us (94%)
  local copies, waits for them, and re-layouts  3.39 us (4%)
  between operations  1.29 us (1%)
    pallas_call x1, Pallas kernels, per_device(): pl.pallas_call(functools.partial(kernel, n_shot, n_tile), out_shape=(pltp...  82.4 us
    unnamed x3, local copies, waits for them, and re-layouts  3.39 us

profile of v2, /device:TPU:96, one launch (start us, length us, event | category | flops | bytes accessed | tf_op | source)
XLA Modules:
  0.0 87.0 jit_solution(13654851467460662170)
XLA Ops:
  1.3 82.4 %shard_map.94 = (f32[3,2,128,128]{3,2,1,0:T(8,128)S(1)}, f32[1,2,16,128,128]{4,3,2,1,0:T(8,128)S(1)}, f32[1,2,16,128,128]{4,3,2,1,0:T(8,128)S(1)}) custom-call(f32[3,2,128,128]{3,2,1,0:T(8,128)} %coefs.1, f32[1,4,16,128,128]{4,3,2,1,0:T(8,128)} %fwd_state.1, f32[1,4,16,128,128]{4,3,2,1,0:T(8,128)} %adj_state.1, s32[1,1]{1,0:T(1,128)S(6)} %copy.16.src_cell, ...), custom_call_target="tpu_custom_call" | custom-call | tf_op jit(solution)/shard_map/pallas_call | solution.py:693
  83.6 0.7 copy.13
  84.4 1.3 %copy.14 = f32[1,2,16,128,128]{4,3,2,1,0:T(8,128)} copy(f32[1,2,16,128,128]{4,3,2,1,0:T(8,128)S(1)} %get-tuple-element.4) | data formatting | bytes 4194304
  85.7 1.3 %copy.15 = f32[1,2,16,128,128]{4,3,2,1,0:T(8,128)} copy(f32[1,2,16,128,128]{4,3,2,1,0:T(8,128)S(1)} %get-tuple-element.5) | data formatting | bytes 4194304

commit v3 on v2

--- a/solution.py
+++ b/solution.py
@@ -358,24 +358,28 @@
                 ff[d + e, r : r + 8] = c * (a * lam + b * mu)
                 oo[d + e + 2, at] = c * (b * lam + mu)
 
-    def forward_group(n, cur, i, group, slot):
+    def forward_group(n, cur, i, group, slot, between=None):
         d = group * DEEP
+        near = d + 2 * core
+        other = d + 2 - 2 * core
         for e in range(DEEP):
             land_rows(pp, cur * AZ + d + e, slot, i * DEEP + e)
         after = (cur + (i + 1) // GROUPS) % 2
         obs_at = jnp.maximum(n - 1, 0)
-        flat_terms(pp, cur, d + 2, terms_b, None)
+        flat_terms(pp, cur, other, terms_b, None)
         for j in range(16):
             gather_row(n, cur, i * 32 + j, obs_at)
-        forward_pair(n, cur, d, terms_a)
-        flat_terms(pp, after, ring_place((i + 1) % GROUPS) * DEEP, terms_a, None)
+        forward_pair(n, cur, near, terms_a)
+        if between is not None:
+            between()
+        flat_terms(pp, after, ring_place((i + 1) % GROUPS) * DEEP + 2 * core, terms_a, None)
         for j in range(16, 32):
             gather_row(n, cur, i * 32 + j, obs_at)
-        forward_pair(n, cur, d + 2, terms_b)
+        forward_pair(n, cur, other, terms_b)
         for e in range(DEEP):
             stage_rows(pp, (1 - cur) * AZ + d + e, 1 - cur, i * DEEP + e)
 
-    flat_terms(pp, 0, ring_place(0) * DEEP, terms_a, None)
+    flat_terms(pp, 0, ring_place(0) * DEEP + 2 * core, terms_a, None)
     observed_load.wait()
     for i in range(1, 8):
         loads[i].wait()
@@ -409,12 +413,17 @@
             pass_far0.start()
             got_hop_down.wait_recv()
             pass_far1.start()
-            via_far0.wait_recv()
-            via_far1.wait_recv()
 
         group = ring_place(i)
         d = group * DEEP
-        forward_group(0, 0, i, group, 3)
+
+        def passed_on():
+            @pl.when(i == 3)
+            def _():
+                via_far0.wait_recv()
+                via_far1.wait_recv()
+
+        forward_group(0, 0, i, group, 3, passed_on)
         ready(1, i)
         scaled_pair(d)
         scaled_pair(d + 2)
@@ -514,7 +523,7 @@
     def last_place(i):
         return (chip + 2 + i - 3 * (i // 2) - 2 * (i // 3)) % GROUPS
 
-    def adj_group(s, cur, i, mode, place):
+    def adj_group(s, cur, i, mode, place, between=None):
         group = place(i)
         d = group * DEEP
         slot = 4 + cur
@@ -526,10 +535,13 @@
 
         for e in range(DEEP):
             land_rows(ff, cur * AZ + d + e, slot, order * DEEP + e)
-        flat_terms(ff, cur, d + 2, terms_b, cur)
-        adj_pair(s, cur, d, terms_a, mode)
-        flat_terms(ff, cur, place((i + 1) % GROUPS) * DEEP, terms_a, cur)
-        adj_pair(s, cur, d + 2, terms_b, mode)
+        lead = 2 - 2 * core
+        flat_terms(ff, cur, d + 2 * core, terms_b, cur)
+        adj_pair(s, cur, d + lead, terms_a, mode)
+        if between is not None:
+            between()
+        flat_terms(ff, cur, place((i + 1) % GROUPS) * DEEP + lead, terms_a, cur)
+        adj_pair(s, cur, d + 2 * core, terms_b, mode)
         if mode != "last":
             for e in range(DEEP):
                 stage_rows(ff, (1 - cur) * AZ + d + e, 5 - cur, i * DEEP + e)
@@ -538,7 +550,7 @@
     def adj_step(s, mode, carry):
         cur = s % 2
         set_spread(STEPS - s, cur)
-        flat_terms(ff, cur, ring_place(0) * DEEP, terms_a, cur)
+        flat_terms(ff, cur, ring_place(0) * DEEP + 2 - 2 * core, terms_a, cur)
 
         def one_group(i, carry):
             adj_group(s, cur, i, mode, ring_place)
@@ -602,7 +614,7 @@
     to_down2 = ring(5, below + 1, down)
 
     set_spread(1, 1)
-    flat_terms(ff, 1, last_place(0) * DEEP, terms_a, 1)
+    flat_terms(ff, 1, last_place(0) * DEEP + 2 - 2 * core, terms_a, 1)
 
     def swap(i):
         return exchange(i, last_place(i))
@@ -613,23 +625,19 @@
         add_pair(i, last_place(i))
 
     def last_group(i, carry):
-        adj_group(5, 1, i, "last", last_place)
-        swap(i).start()
-
-        @pl.when(i > 0)
-        def _():
-            summed(i - 1)
-
-        @pl.when(i == 1)
+        adj_group(5, 1, i, "last", last_place, lambda: swap(i).start())
+        summed(i)
+
+        @pl.when(i == 0)
         def _():
             to_up0.start()
             to_down0.start()
 
+        @pl.when(i == 1)
+        def _():
+            to_down1.start()
+
         @pl.when(i == 2)
-        def _():
-            to_down1.start()
-
-        @pl.when(i == 3)
         def _():
             to_up1.start()
 
@@ -640,7 +648,6 @@
     out_m = pltpu.make_async_copy(mm.at[0:AZ], adj_final.at[0, 1], out_sem.at[3])
     out_l.start()
     out_m.start()
-    summed(GROUPS - 1)
     to_up0.wait_recv()
     add_hop(0, above)
     to_up2.start()

time: 87.2 us -> 87.3 us (level)
  no operation moved by 1% of the time
where the time goes in v3:
time: 87.3 us; the launch traced here: 87.2 us
  Pallas kernels  82.5 us (95%)
  local copies, waits for them, and re-layouts  3.39 us (4%)
  between operations  1.29 us (1%)
    pallas_call x1, Pallas kernels, per_device(): pl.pallas_call(functools.partial(kernel, n_shot, n_tile), out_shape=(pltp...  82.5 us
    unnamed x3, local copies, waits for them, and re-layouts  3.39 us

profile of v3, /device:TPU:96, one launch (start us, length us, event | category | flops | bytes accessed | tf_op | source)
XLA Modules:
  0.0 87.2 jit_solution(895905784387330284)
XLA Ops:
  1.3 82.5 %shard_map.94 = (f32[3,2,128,128]{3,2,1,0:T(8,128)S(1)}, f32[1,2,16,128,128]{4,3,2,1,0:T(8,128)S(1)}, f32[1,2,16,128,128]{4,3,2,1,0:T(8,128)S(1)}) custom-call(f32[3,2,128,128]{3,2,1,0:T(8,128)} %coefs.1, f32[1,4,16,128,128]{4,3,2,1,0:T(8,128)} %fwd_state.1, f32[1,4,16,128,128]{4,3,2,1,0:T(8,128)} %adj_state.1, s32[1,1]{1,0:T(1,128)S(6)} %copy.16.src_cell, ...), custom_call_target="tpu_custom_call" | custom-call | tf_op jit(solution)/shard_map/pallas_call | solution.py:700
  83.8 0.7 copy.13
  84.5 1.3 %copy.14 = f32[1,2,16,128,128]{4,3,2,1,0:T(8,128)} copy(f32[1,2,16,128,128]{4,3,2,1,0:T(8,128)S(1)} %get-tuple-element.4) | data formatting | bytes 4194304
  85.8 1.3 %copy.15 = f32[1,2,16,128,128]{4,3,2,1,0:T(8,128)} copy(f32[1,2,16,128,128]{4,3,2,1,0:T(8,128)S(1)} %get-tuple-element.5) | data formatting | bytes 4194304
